TPU v7x, 1024 devices: a whole 4x8x16 slice. The times are simulated.
1024 devices in a mesh: dp: 32 (over y, x), expert: 32 (over z, core).
Axes of the slice: x: 4, y: 8, z: 16, core: 2. Of those that a mesh axis runs over, the one named last changes fastest.
Arguments:
- tokens: bfloat16 [131072, 2048], P(('dp', 'expert')), may hold values from -6 to 6
- expert_ids: int32 [131072, 8], P(('dp', 'expert')), may hold values from 0 to 127, as said below
- gate_weights: float32 [131072, 8], P(('dp', 'expert')), may hold values from 0.1 to 1
- cotangent: bfloat16 [131072, 2048], P(('dp', 'expert')), may hold values from -3 to 3
- w_in: bfloat16 [2, 3072, 2048], P(None, 'expert'), may hold values from -0.125 to 0.125
- w_down: bfloat16 [3072, 2048], P('expert'), may hold values from -0.15625 to 0.15625
Outputs:
- moe_out: bfloat16 [131072, 2048], P(('dp', 'expert'))
- grad_tokens: bfloat16 [131072, 2048], P(('dp', 'expert'))
- grad_w_in: float32 [2, 3072, 2048], P(None, ('expert', 'dp'))
- grad_w_down: float32 [3072, 2048], P(('expert', 'dp'))
Inputs may be any that keep to these rules, and one draw needn't show every extreme that they name: `expert_ids`: each token names 8 different experts, at most one of them below 2. In the 128 rows of one device no expert below 2 is named more than 8 times, and in every draw one expert below 2 is named exactly 8 times in the rows of every device.
All inputs are finite; a program needn't handle non-finite values.
Results may differ from a plain program's by a relative error of at most 0.02.
Values may be sent and summed in bfloat16 or wider, within the bound.
A program may use at most 32 MiB of HBM per device.

v0:
```python
import jax
import jax.numpy as jnp
from jax import lax
from jax.sharding import PartitionSpec as P

EXP_WIN = 2
CAP = 8


def silu_grad(preact):
    logistic = jax.nn.sigmoid(preact)
    return logistic * (1.0 + preact * (1.0 - logistic))


def per_device(tokens, expert_ids, gate_weights, cotangent, w_in, w_down):
    devices_on = lax.axis_size("expert")
    features = tokens.shape[1]
    hidden_dev = w_down.shape[0]
    experts_held = EXP_WIN
    sharers = devices_on // experts_held
    capacity = CAP
    wanted = jnp.arange(experts_held, dtype=jnp.int32)
    matches = expert_ids[None, :, :] == wanted[:, None, None]
    chosen = jnp.any(matches, axis=2)
    weight = jnp.sum(jnp.where(matches, gate_weights[None, :, :], 0.0), axis=2)
    slot_rank = jnp.cumsum(chosen.astype(jnp.int32), axis=1) - 1
    slot_ids = jnp.arange(capacity, dtype=jnp.int32)
    picker = chosen[:, None, :] & (slot_rank[:, None, :] == slot_ids[None, :, None])
    pick_bf = picker.astype(jnp.bfloat16)
    token_slots = jnp.einsum(
        "ect,td->ecd", pick_bf, tokens, preferred_element_type=jnp.float32
    ).astype(jnp.bfloat16)
    cotan_slots = jnp.einsum("ect,td->ecd", pick_bf, cotangent, preferred_element_type=jnp.float32)
    gate_slots = jnp.sum(jnp.where(picker, weight[:, None, :], 0.0), axis=2)
    weighted_slots = (gate_slots[:, :, None] * cotan_slots).astype(jnp.bfloat16)
    send_rows = jnp.broadcast_to(
        token_slots[:, None], (experts_held, sharers, capacity, features)
    ).reshape(devices_on * capacity, features)
    send_cotan = jnp.broadcast_to(
        weighted_slots[:, None], (experts_held, sharers, capacity, features)
    ).reshape(devices_on * capacity, features)
    recv_rows, recv_cotan = (
        lax.all_to_all(send_rows, "expert", split_axis=0, concat_axis=0, tiled=True),
        lax.all_to_all(send_cotan, "expert", split_axis=0, concat_axis=0, tiled=True),
    )
    contract_last = (((1,), (1,)), ((), ()))
    w_in_flat = w_in.reshape(2 * hidden_dev, features)
    projected = lax.dot_general(
        recv_rows, w_in_flat, contract_last, preferred_element_type=jnp.float32
    )
    gate_pre = projected[:, :hidden_dev]
    up_pre = projected[:, hidden_dev:]
    hidden = (jax.nn.silu(gate_pre) * up_pre).astype(jnp.bfloat16)
    out_part = jnp.dot(hidden, w_down, preferred_element_type=jnp.float32).astype(jnp.bfloat16)
    grad_hidden = lax.dot_general(
        recv_cotan, w_down, contract_last, preferred_element_type=jnp.float32
    )
    grad_gate = (grad_hidden * up_pre * silu_grad(gate_pre)).astype(jnp.bfloat16)
    grad_up = (grad_hidden * jax.nn.silu(gate_pre)).astype(jnp.bfloat16)
    grad_pre = jnp.concatenate([grad_gate, grad_up], axis=1)
    grad_part = jnp.dot(grad_pre, w_in_flat, preferred_element_type=jnp.float32).astype(
        jnp.bfloat16
    )
    returned_out, returned_grad = (
        lax.all_to_all(out_part, "expert", split_axis=0, concat_axis=0, tiled=True),
        lax.all_to_all(grad_part, "expert", split_axis=0, concat_axis=0, tiled=True),
    )
    contract_rows = (((0,), (0,)), ((), ()))
    gate_term = lax.dot_general(
        grad_gate, recv_rows, contract_rows, preferred_element_type=jnp.float32
    )
    up_term = lax.dot_general(grad_up, recv_rows, contract_rows, preferred_element_type=jnp.float32)
    down_term = lax.dot_general(
        hidden, recv_cotan, contract_rows, preferred_element_type=jnp.float32
    )
    grad_shard = lax.psum_scatter(
        jnp.concatenate([gate_term, up_term, down_term], axis=1).astype(jnp.bfloat16),
        "dp",
        scatter_dimension=0,
        tiled=True,
    ).astype(jnp.float32)
    out_sum = jnp.sum(
        returned_out.astype(jnp.float32).reshape(experts_held, sharers, capacity, features), axis=1
    )
    out_sum = out_sum * gate_slots[:, :, None]
    grad_sum_rows = jnp.sum(
        returned_grad.astype(jnp.float32).reshape(experts_held, sharers, capacity, features), axis=1
    )
    pick_f = picker.astype(jnp.float32)
    moe_out = jnp.einsum("ect,ecd->td", pick_f, out_sum, precision=lax.Precision.HIGHEST).astype(
        jnp.bfloat16
    )
    grad_tokens = jnp.einsum(
        "ect,ecd->td", pick_f, grad_sum_rows, precision=lax.Precision.HIGHEST
    ).astype(jnp.bfloat16)
    grad_w_in = jnp.stack(
        [grad_shard[:, :features], grad_shard[:, features : 2 * features]], axis=0
    )
    grad_w_down = grad_shard[:, 2 * features :]
    return (moe_out, grad_tokens, grad_w_in, grad_w_down)


def solution(mesh):
    in_specs = (
        P(("dp", "expert"), None),
        P(("dp", "expert"), None),
        P(("dp", "expert"), None),
        P(("dp", "expert"), None),
        P(None, "expert", None),
        P("expert", None),
    )
    out_specs = (
        P(("dp", "expert"), None),
        P(("dp", "expert"), None),
        P(None, ("expert", "dp"), None),
        P(("expert", "dp"), None),
    )
    return jax.shard_map(
        per_device, mesh=mesh, in_specs=in_specs, out_specs=out_specs, check_vma=False
    )
```

profile of v0, /device:TPU:8, one launch (start us, length us, event | category | flops | bytes accessed | tf_op | source)
XLA Modules:
  0.0 415.0 jit_solution(1640511080962948398)
XLA Ops:
  7.2 0.8 fusion.20
  8.3 1.2 convolution_convert_fusion.5
  9.5 1.1 broadcast_in_dim.28
  10.6 19.3 %all-to-all-start = ((bf16[32,8,2048]{2,1,0:T(8,128)(2,1)}), bf16[32,8,2048]{2,1,0:T(8,128)(2,1)S(1)}, u32[]{:S(2)}, u32[]{:S(2)}) async-start(bf16[32,8,2048]{2,1,0:T(8,128)(2,1)} %bitcast.1), calls=%async_computation | async-start | bytes 2097152 | tf_op jit(solution)/shard_map/all_to_all | solution.py:43
  30.2 55.7 %all-to-all-done = bf16[32,8,2048]{2,1,0:T(8,128)(2,1)S(1)} async-done(((bf16[32,8,2048]{2,1,0:T(8,128)(2,1)}), bf16[32,8,2048]{2,1,0:T(8,128)(2,1)S(1)}, u32[]{:S(2)}, u32[]{:S(2)}) %all-to-all-start) | async-done | bytes 1048608 | tf_op jit(solution)/shard_map/all_to_all | solution.py:43
  85.9 1.1 broadcast_in_dim.50
  87.0 3.9 all-to-all-start.2
  90.9 0.5 fusion.10
  91.5 56.0 %all-to-all-done.2 = bf16[32,8,2048]{2,1,0:T(8,128)(2,1)S(1)} async-done(((bf16[32,8,2048]{2,1,0:T(8,128)(2,1)}), bf16[32,8,2048]{2,1,0:T(8,128)(2,1)S(1)}, u32[]{:S(2)}, u32[]{:S(2)}) %all-to-all-start.2) | async-done | bytes 1048608 | tf_op jit(solution)/shard_map/all_to_all | solution.py:44
  147.9 0.6 copy-done.5
  148.5 1.4 fusion
  150.0 3.9 all-to-all-start.3
  153.9 1.4 fusion.1
  155.7 54.7 %all-to-all-done.3 = bf16[32,8,2048]{2,1,0:T(8,128)(2,1)S(1)} async-done(((bf16[32,8,2048]{2,1,0:T(8,128)(2,1)}), bf16[32,8,2048]{2,1,0:T(8,128)(2,1)S(1)}, u32[]{:S(2)}, u32[]{:S(2)}) %all-to-all-start.3) | async-done | bytes 1048608 | tf_op jit(solution)/shard_map/all_to_all | solution.py:66
  210.4 4.7 %all-to-all-start.1 = ((bf16[32,8,2048]{2,1,0:T(8,128)(2,1)}), bf16[32,8,2048]{2,1,0:T(8,128)(2,1)}, u32[]{:S(2)}, u32[]{:S(2)}) async-start(bf16[32,8,2048]{2,1,0:T(8,128)(2,1)} %fusion.1), calls=%async_computation.1 | async-start | bytes 2097152 | tf_op jit(solution)/shard_map/all_to_all | solution.py:65
  216.2 1.1 pad_maximum_fusion
  217.3 1.3 dynamic-slice
  219.3 182.2 %all-reduce.3.cloned.1.call-done = bf16[96,6144]{1,0:T(8,128)(2,1)} async-done(((bf16[96,6144]{1,0:T(8,128)(2,1)}), bf16[96,6144]{1,0:T(8,128)(2,1)}) %all-reduce.3.cloned.1.call-update) | async-done | bytes 1179664
  401.5 1.0 dynamic-slice_convert_fusion
  402.5 0.6 fusion.35
  403.1 0.7 copy.16
  403.9 1.4 fusion.3
  405.3 1.4 convert_reduce_fusion.1
  406.7 1.4 fusion.2
  (36 shorter events, 2.7 us)
Async XLA Ops:
  7.2 83.7 %copy-start = (bf16[2,96,2048]{2,1,0:T(8,128)(2,1)S(1)}, bf16[2,96,2048]{2,1,0:T(8,128)(2,1)}, u32[]{:S(2)}) copy-start(bf16[2,96,2048]{2,1,0:T(8,128)(2,1)} %param.10) | copy-start | bytes 2359300
  10.6 19.3 %copy-start.9 = (s32[128,8]{0,1:T(8,128)S(1)}, s32[128,8]{0,1:T(8,128)}, u32[]{:S(2)}) copy-start(s32[128,8]{0,1:T(8,128)} %param.7) | copy-start | bytes 12292
  10.6 19.3 %copy-start.10 = (f32[128,8]{0,1:T(8,128)S(1)}, f32[128,8]{0,1:T(8,128)}, u32[]{:S(2)}) copy-start(f32[128,8]{0,1:T(8,128)} %param.8) | copy-start | bytes 12292
  10.6 19.4 %copy-start.3 = (bf16[128,2048]{1,0:T(8,128)(2,1)S(1)}, bf16[128,2048]{1,0:T(8,128)(2,1)}, u32[]{:S(2)}) copy-start(bf16[128,2048]{1,0:T(8,128)(2,1)} %param.9) | copy-start | bytes 1572868
  10.6 75.3 %all-to-all-start = ((bf16[32,8,2048]{2,1,0:T(8,128)(2,1)}), bf16[32,8,2048]{2,1,0:T(8,128)(2,1)S(1)}, u32[]{:S(2)}, u32[]{:S(2)}) async-start(bf16[32,8,2048]{2,1,0:T(8,128)(2,1)} %bitcast.1), calls=%async_computation | async-start | bytes 2097152 | tf_op jit(solution)/shard_map/all_to_all | solution.py:43
  87.0 60.4 %all-to-all-start.2 = ((bf16[32,8,2048]{2,1,0:T(8,128)(2,1)}), bf16[32,8,2048]{2,1,0:T(8,128)(2,1)S(1)}, u32[]{:S(2)}, u32[]{:S(2)}) async-start(bf16[32,8,2048]{2,1,0:T(8,128)(2,1)} %bitcast.57), calls=%async_computation.2 | async-start | bytes 2097152 | tf_op jit(solution)/shard_map/all_to_all | solution.py:44
  90.9 56.5 %copy-start.4 = (bf16[96,2048]{1,0:T(8,128)(2,1)S(1)}, bf16[96,2048]{1,0:T(8,128)(2,1)}, u32[]{:S(2)}) copy-start(bf16[96,2048]{1,0:T(8,128)(2,1)} %param.11) | copy-start | bytes 1179652
  147.4 2.6 copy-start.1
  147.9 0.6 copy-start.5
  147.9 0.6 copy-start.7
  150.0 60.4 %all-to-all-start.3 = ((bf16[32,8,2048]{2,1,0:T(8,128)(2,1)}), bf16[32,8,2048]{2,1,0:T(8,128)(2,1)S(1)}, u32[]{:S(2)}, u32[]{:S(2)}) async-start(bf16[32,8,2048]{2,1,0:T(8,128)(2,1)} %fusion), calls=%async_computation.3 | async-start | bytes 2097152 | tf_op jit(solution)/shard_map/all_to_all | solution.py:66
  153.9 1.4 copy-start.2
  155.7 59.5 %copy-start.8 = (bf16[256,96]{0,1:T(8,128)(2,1)S(1)}, bf16[256,96]{0,1:T(8,128)(2,1)}, u32[]{:S(2)}) copy-start(bf16[256,96]{0,1:T(8,128)(2,1)} %copy-done.7) | copy-start | bytes 147460
  210.4 194.9 %all-to-all-start.1 = ((bf16[32,8,2048]{2,1,0:T(8,128)(2,1)}), bf16[32,8,2048]{2,1,0:T(8,128)(2,1)}, u32[]{:S(2)}, u32[]{:S(2)}) async-start(bf16[32,8,2048]{2,1,0:T(8,128)(2,1)} %fusion.1), calls=%async_computation.1 | async-start | bytes 2097152 | tf_op jit(solution)/shard_map/all_to_all | solution.py:65
  215.1 0.8 copy-start.6
  215.1 186.4 %all-reduce.3.cloned.1.call-start = ((), (), s32[]{:S(2)}) async-start(), calls=%async_computation.4 | async-start | bytes 2359296
Sparse Core Ops, SparseCore 0:
  219.3 182.1 all-reduce.2
where the time goes:
time: 416 us; the launch traced here: 415 us
  waiting for transfers between devices  349 us (84%)
  starting transfers between devices  31.8 us (8%)
  between operations  14.9 us (4%)
  matrix products  8.99 us (2%)
  local copies, waits for them, and re-layouts  5.85 us (1%)
  other arithmetic  4.83 us (1%)
    unnamed x2, waiting for transfers between devices  182 us
    all_to_all x1, waiting for transfers between devices, per_device(): lax.all_to_all(send_cotan, 'expert', split_axis=0, concat_axis=0, tiled=T...  56 us
    all_to_all x1, waiting for transfers between devices, per_device(): lax.all_to_all(send_rows, 'expert', split_axis=0, concat_axis=0, tiled=True)  55.7 us
    all_to_all x1, waiting for transfers between devices, per_device(): lax.all_to_all(grad_part, 'expert', split_axis=0, concat_axis=0, tiled=True)  54.7 us
    all_to_all x1, starting transfers between devices, per_device(): lax.all_to_all(send_rows, 'expert', split_axis=0, concat_axis=0, tiled=True)  19.3 us
  transfers between devices with their start and end apart: 5, of which 4 were waited for; matrix products, arithmetic and copies ran while one was open for 2% of the time, Pallas kernels for 0%

commit v1 on v0

v1 whole, which is shorter than its diff:
```python
import functools

import jax
import jax.numpy as jnp
from jax import lax
from jax.experimental import pallas as pl
from jax.experimental.pallas import tpu as pltpu
from jax.sharding import PartitionSpec as P

MESH = pl.DeviceIdType.MESH
F32 = jnp.float32
BF16 = jnp.bfloat16
NT = (((1,), (1,)), ((), ()))
TN = (((0,), (0,)), ((), ()))


def moe_kernel(
    n_dp, nz,
    ids_ref, gates_ref, tok_hbm, cot_hbm, win_hbm, wdn_hbm,
    out_ref, gtok_ref, gwin_ref, gwdn_ref,
    tok, cot, win, wdn, x, pre, p32, q, qr, sb, rb, g32, g, rg, acc9,
    in_sem, ag_send, ag_recv, sib_send, sib_recv, q_send, q_recv,
    rs_send, rs_recv, g_send, g_recv,
):
    half = nz // 2
    feats = tok.shape[1]
    blocks = feats // 128
    hid = wdn.shape[0]
    per = hid // n_dp
    ntok = tok.shape[0]
    dp = lax.axis_index("dp")
    ex = lax.axis_index("expert")
    z = lax.div(ex, 2)
    core = lax.rem(ex, 2)
    zz = lax.rem(z, half)
    zl = half - 1 - zz
    held = lax.div(z, half)
    right = (dp, lax.rem(z + 1, nz) * 2 + core)
    left = (dp, lax.rem(z + nz - 1, nz) * 2 + core)
    sib = (dp, z * 2 + 1 - core)

    loads = [
        pltpu.make_async_copy(tok_hbm, tok, in_sem.at[0]),
        pltpu.make_async_copy(cot_hbm, cot, in_sem.at[1]),
        pltpu.make_async_copy(win_hbm, win, in_sem.at[2]),
        pltpu.make_async_copy(wdn_hbm, wdn, in_sem.at[3]),
    ]
    for load in loads:
        load.start()

    barrier = pltpu.get_barrier_semaphore()
    for dev in (right, left, sib):
        pl.semaphore_signal(barrier, inc=1, device_id=dev, device_id_type=MESH)

    @pl.loop(1, n_dp)
    def _(k):
        pl.semaphore_signal(
            barrier, inc=1, device_id=(lax.rem(dp + k, n_dp), ex), device_id_type=MESH
        )

    ids = ids_ref[...]
    gates = gates_ref[...]
    lane = lax.broadcasted_iota(jnp.int32, (ntok, ntok), 1)
    sub = lax.broadcasted_iota(jnp.int32, (ntok, ntok), 0)
    tri = jnp.where(lane < sub, 1.0, 0.0).astype(BF16)
    table = jnp.zeros((ntok, ntok), F32)
    for e in range(2):
        hit = ids == e
        chosen = jnp.max(jnp.where(hit, 1.0, 0.0), axis=1, keepdims=True)
        weight = jnp.sum(jnp.where(hit, gates, 0.0), axis=1, keepdims=True)
        table = jnp.where(lane == e, chosen, table)
        table = jnp.where(lane == 2 + e, weight, table)
    ranks = jnp.dot(tri, table.astype(BF16), preferred_element_type=F32)
    table_t = jnp.transpose(table)
    ranks_t = jnp.transpose(ranks)
    slot = lax.broadcasted_iota(jnp.int32, (8, ntok), 0).astype(F32)
    picks = []
    scales = []
    for e in range(2):
        pick = jnp.where(
            (table_t[e:e + 1] > 0.5) & (ranks_t[e:e + 1] == slot), 1.0, 0.0
        )
        picks.append(pick)
        scales.append(jnp.sum(pick * table_t[2 + e:3 + e], axis=1, keepdims=True))
    pick = jnp.concatenate(picks, axis=0).astype(BF16)
    scale = jnp.concatenate(scales, axis=0)

    loads[0].wait()
    tok_rows = jnp.dot(pick, tok[...], preferred_element_type=F32)
    loads[1].wait()
    cot_rows = jnp.dot(pick, cot[...], preferred_element_type=F32) * scale
    packet = [
        jnp.concatenate([tok_rows[8 * e:8 * e + 8], cot_rows[8 * e:8 * e + 8]], axis=0)
        for e in range(2)
    ]
    first = held == 0
    x[0, 0] = jnp.where(first, packet[0], packet[1]).astype(BF16)
    x[2, 0] = jnp.where(first, packet[1], packet[0]).astype(BF16)

    pl.semaphore_wait(barrier, 3 + n_dp - 1)

    def slot_r(i):
        return 2 * i - 1 if i > 0 else 0

    def slot_l(i):
        return 2 * i

    def slot_of(d, i):
        return slot_r(i) if d == 0 else slot_l(i)

    steps = (half, half - 1)
    edge = (zz, zl)
    toward = (right, left)

    def ag_copy(d, kind, i, at_edge):
        src = x.at[2 * kind, slot_of(d, i - 1)]
        land = 1 - kind if at_edge else kind
        return pltpu.make_async_remote_copy(
            src_ref=src,
            dst_ref=x.at[2 * land, slot_of(d, i)],
            send_sem=ag_send.at[d, kind, i],
            recv_sem=ag_recv.at[d, land, i],
            device_id=toward[d],
            device_id_type=MESH,
        )

    def other_limit(d):
        return edge[d] + 1 if d == 0 else edge[d]

    def ag_own(d, i, act):
        @pl.when(edge[d] <= half - 2)
        def _():
            act(ag_copy(d, 0, i, False))

    def ag_other(d, i, act):
        @pl.when((edge[d] <= half - 2) & (i <= other_limit(d)))
        def _():
            act(ag_copy(d, 1, i, False))

        @pl.when((edge[d] == half - 1) & (i <= other_limit(d)))
        def _():
            act(ag_copy(d, 1, i, True))

    def start(copy):
        copy.start()

    def wait_send(copy):
        copy.wait_send()

    def ag_wait(d, kind, i):
        pltpu.make_async_remote_copy(
            src_ref=x.at[2 * kind, slot_of(d, i)],
            dst_ref=x.at[2 * kind, slot_of(d, i)],
            send_sem=ag_send.at[d, kind, i],
            recv_sem=ag_recv.at[d, kind, i],
            device_id=toward[d],
            device_id_type=MESH,
        ).wait_recv()

    def sib_copy(s):
        return pltpu.make_async_remote_copy(
            src_ref=x.at[0, s],
            dst_ref=x.at[1, s],
            send_sem=sib_send.at[s],
            recv_sem=sib_recv.at[s],
            device_id=sib,
            device_id_type=MESH,
        )

    per_batch = 4 if nz % 4 == 0 else 2
    batches = nz // per_batch
    rows = per_batch * 16

    def stage_one(b):
        lo = b * per_batch
        for s in range(lo, lo + per_batch):
            sib_copy(s).wait_recv()
        xb = x[0:2, lo:lo + per_batch].reshape(2 * rows, feats)
        gate = lax.dot_general(xb, win[0], NT, preferred_element_type=F32)
        up = lax.dot_general(xb, win[1], NT, preferred_element_type=F32)
        grad = lax.dot_general(xb, wdn[...], NT, preferred_element_type=F32)
        gate = gate.reshape(2 * per_batch, 16, hid)[:, 0:8]
        up = up.reshape(2 * per_batch, 16, hid)[:, 0:8]
        grad = grad.reshape(2 * per_batch, 16, hid)[:, 8:16]
        sig = 1.0 / (1.0 + jnp.exp(-gate))
        silu = gate * sig
        hidden = silu * up
        grad_gate = grad * up * (sig * (1.0 + gate * (1.0 - sig)))
        grad_up = grad * silu
        zero = jnp.zeros_like(hidden)
        for k, pair in enumerate(
            ((grad_gate, zero), (grad_up, zero), (zero, hidden))
        ):
            both = jnp.concatenate(pair, axis=1).astype(BF16)
            pre[k, 0:2, lo:lo + per_batch] = both.reshape(2, per_batch, 16, hid)
        for k, pair in enumerate(
            ((zero, grad_gate), (zero, grad_up), (hidden, zero))
        ):
            both = jnp.concatenate(pair, axis=1).astype(BF16)
            pre[3 + k, 0:2, lo:lo + per_batch] = both.reshape(2, per_batch, 16, hid)

    for kind in (1, 0):
        for d in (0, 1):
            (ag_own if kind == 0 else ag_other)(d, 1, start)
    sib_copy(0).start()
    for load in loads[2:]:
        load.wait()
    done = 0
    for i in range(1, half + 1):
        for d in (0, 1):
            if i > steps[d]:
                continue
            ag_wait(d, 0, i)
            if i < steps[d]:
                ag_own(d, i + 1, start)
            sib_copy(slot_of(d, i)).start()

            @pl.when((i <= other_limit(d) - 1) & (i <= steps[d]))
            def _():
                ag_wait(d, 1, i)

            if i < steps[d]:
                ag_other(d, i + 1, start)
        if i < half and 2 * i - 1 >= (done + 1) * per_batch:
            stage_one(done)
            done += 1
    while done < batches:
        stage_one(done)
        done += 1

    def q_copy(b):
        lo = b * per_batch
        return pltpu.make_async_remote_copy(
            src_ref=q.at[pl.ds(lo, per_batch)],
            dst_ref=qr.at[pl.ds(lo, per_batch)],
            send_sem=q_send.at[b],
            recv_sem=q_recv.at[b],
            device_id=sib,
            device_id_type=MESH,
        )

    def stage_two(b):
        lo = b * per_batch
        for c in (1, 0):
            total = None
            for k, w in enumerate((win.at[0], win.at[1], wdn)):
                lhs = pre[3 + k, c, lo:lo + per_batch].reshape(rows, hid)
                term = jnp.dot(lhs, w[...], preferred_element_type=F32)
                total = term if total is None else total + term
            total = total.reshape(per_batch, 16, feats)
            if c == 1:
                q[lo:lo + per_batch] = total.astype(BF16)
                q_copy(b).start()
            else:
                p32[lo:lo + per_batch] = total

    def rs_copy(d, kind, i):
        slot = slot_of(d, i)
        crossing = zz == 0 if d == 0 else zl == 0
        src = sb.at[slot] if kind == 0 else rb.at[d, 1, i]

        def make(land):
            return pltpu.make_async_remote_copy(
                src_ref=src,
                dst_ref=rb.at[d, land, i - 1],
                send_sem=rs_send.at[d, kind, i],
                recv_sem=rs_recv.at[d, land, i - 1],
                device_id=toward[1 - d],
                device_id_type=MESH,
            )

        return crossing, make

    def rs_own(d, i, act):
        crossing, make = rs_copy(d, 0, i)

        @pl.when(crossing)
        def _():
            act(make(1))

        @pl.when(jnp.logical_not(crossing))
        def _():
            act(make(0))

    def rs_other(d, i, act):
        _, make = rs_copy(d, 1, i)

        @pl.when(edge[1 - d] < steps[d] - i)
        def _():
            act(make(1))

    def rs_wait(d, kind, i):
        pltpu.make_async_remote_copy(
            src_ref=rb.at[d, kind, i],
            dst_ref=rb.at[d, kind, i],
            send_sem=rs_send.at[d, kind, i],
            recv_sem=rs_recv.at[d, kind, i],
            device_id=toward[1 - d],
            device_id_type=MESH,
        ).wait_recv()

    def chain(d, i):
        slot = slot_of(d, i)
        if i < steps[d]:
            @pl.when(edge[1 - d] < steps[d] - i)
            def _():
                rs_wait(d, 1, i)

            rs_other(d, i, start)
            has = edge[1 - d] >= 1

            @pl.when(has)
            def _():
                rs_wait(d, 0, i)
                sb[slot] = (
                    p32[slot] + qr[slot].astype(F32) + rb[d, 0, i].astype(F32)
                ).astype(BF16)

            @pl.when(jnp.logical_not(has))
            def _():
                sb[slot] = (p32[slot] + qr[slot].astype(F32)).astype(BF16)
        else:
            sb[slot] = (p32[slot] + qr[slot].astype(F32)).astype(BF16)
        rs_own(d, i, start)

    def g_copy(k):
        peer = lax.rem(dp + k, n_dp)
        return pltpu.make_async_remote_copy(
            src_ref=g.at[peer],
            dst_ref=rg.at[k],
            send_sem=g_send.at[k],
            recv_sem=g_recv.at[k],
            device_id=(peer, ex),
            device_id_type=MESH,
        )

    def g_block(n):
        at = pl.ds(pl.multiple_of(n * 16, 16), 16)
        return jnp.concatenate([g32[kj, at, :] for kj in range(3 * per)], axis=1)

    def weight_grads():
        unit = lax.broadcasted_iota(jnp.int32, (hid, hid), 1)
        row = lax.broadcasted_iota(jnp.int32, (hid, hid), 0)
        want = lax.rem(row, n_dp) * per + lax.div(row, n_dp)
        perm = jnp.where(unit == want, 1.0, 0.0).astype(BF16)
        lhs = jnp.concatenate(
            [
                lax.dot_general(
                    perm, pre[k].reshape(2 * nz * 16, hid), NT, preferred_element_type=F32
                )
                for k in range(3)
            ],
            axis=0,
        ).astype(BF16)
        for r2 in range(blocks // 2):
            xs = x[0:2, :, :, 256 * r2:256 * r2 + 256].reshape(2 * nz * 16, 256)
            term = jnp.dot(lhs, xs, preferred_element_type=F32)
            for r in (0, 1):
                for kj in range(3 * per):
                    g32[kj, pl.ds(2 * r2 + r, n_dp, stride=16), :] = term[
                        kj * n_dp:kj * n_dp + n_dp, 128 * r:128 * r + 128
                    ]

        @pl.loop(1, n_dp)
        def _(k):
            peer = lax.rem(dp + k, n_dp)
            g[peer] = g_block(peer).astype(BF16)
            g_copy(k).start()

    order = list(range(batches - 1, -1, -1))
    stage_two(order[0])
    weight_grads()
    for b in order[1:]:
        stage_two(b)
    arrived = batches
    for j in range(1, half + 1):
        for d in (0, 1):
            i = half + 1 - j if d == 0 else half - j
            if i < 1:
                continue
            while arrived * per_batch > slot_of(d, i):
                arrived -= 1
                q_copy(arrived).wait_recv()
            chain(d, i)
    while arrived > 0:
        arrived -= 1
        q_copy(arrived).wait_recv()

    acc9[...] = g_block(dp)

    @pl.loop(1, n_dp)
    def _(k):
        g_copy(k).wait_recv()
        acc9[...] += rg[k].astype(F32)

    for kj in range(3 * per):
        kind, j = kj // per, kj % per
        for r in range(blocks):
            line = acc9[r:r + 1, kj * 128:kj * 128 + 128]
            if kind < 2:
                gwin_ref[kind, j:j + 1, r * 128:r * 128 + 128] = line
            else:
                gwdn_ref[j:j + 1, r * 128:r * 128 + 128] = line

    p32[0] = p32[0] + qr[0].astype(F32)
    p32[1] = jnp.zeros((16, feats), F32)
    for d in (0, 1):
        @pl.when(edge[1 - d] >= 1)
        def _():
            rs_wait(d, 0, 0)
            p32[0] = p32[0] + rb[d, 0, 0].astype(F32)

        @pl.when(edge[1 - d] < steps[d])
        def _():
            rs_wait(d, 1, 0)
            p32[1] = p32[1] + rb[d, 1, 0].astype(F32)

    mine, theirs = p32[0], p32[1]
    sums = [jnp.where(first, mine, theirs), jnp.where(first, theirs, mine)]
    out_rows = jnp.concatenate([sums[0][0:8], sums[1][0:8]], axis=0) * scale
    grad_rows = jnp.concatenate([sums[0][8:16], sums[1][8:16]], axis=0)
    out_ref[...] = lax.dot_general(
        pick, out_rows.astype(BF16), TN, preferred_element_type=F32
    ).astype(BF16)
    gtok_ref[...] = lax.dot_general(
        pick, grad_rows.astype(BF16), TN, preferred_element_type=F32
    ).astype(BF16)

    for d in (0, 1):
        for i in range(1, steps[d] + 1):
            ag_own(d, i, wait_send)
            ag_other(d, i, wait_send)
            rs_own(d, i, wait_send)
            if i < steps[d]:
                rs_other(d, i, wait_send)
    for s in range(nz):
        sib_copy(s).wait_send()
    for b in range(batches):
        q_copy(b).wait_send()

    @pl.loop(1, n_dp)
    def _(k):
        g_copy(k).wait_send()


def solution(mesh):
    n_dp = mesh.shape["dp"]
    nz = mesh.shape["expert"] // 2

    def step(tokens, expert_ids, gate_weights, cotangent, w_in, w_down):
        ntok, feats = tokens.shape
        hid = w_down.shape[0]
        per = hid // n_dp
        half = nz // 2
        batches = nz // (4 if nz % 4 == 0 else 2)
        vmem = pl.BlockSpec(memory_space=pltpu.VMEM)
        hbm = pl.BlockSpec(memory_space=pl.ANY)
        dma = pltpu.SemaphoreType.DMA
        return pl.pallas_call(
            functools.partial(moe_kernel, n_dp, nz),
            out_shape=(
                jax.ShapeDtypeStruct((ntok, feats), BF16),
                jax.ShapeDtypeStruct((ntok, feats), BF16),
                jax.ShapeDtypeStruct((2, per, feats), F32),
                jax.ShapeDtypeStruct((per, feats), F32),
            ),
            in_specs=[vmem, vmem, hbm, hbm, hbm, hbm],
            out_specs=(vmem, vmem, vmem, vmem),
            scratch_shapes=[
                pltpu.VMEM((ntok, feats), BF16),
                pltpu.VMEM((ntok, feats), BF16),
                pltpu.VMEM((2, hid, feats), BF16),
                pltpu.VMEM((hid, feats), BF16),
                pltpu.VMEM((3, nz, 16, feats), BF16),
                pltpu.VMEM((6, 2, nz, 16, hid), BF16),
                pltpu.VMEM((nz, 16, feats), F32),
                pltpu.VMEM((nz, 16, feats), BF16),
                pltpu.VMEM((nz, 16, feats), BF16),
                pltpu.VMEM((nz, 16, feats), BF16),
                pltpu.VMEM((2, 2, half, 16, feats), BF16),
                pltpu.VMEM((3 * per, n_dp * 16, 128), F32),
                pltpu.VMEM((n_dp, 16, 3 * per * 128), BF16),
                pltpu.VMEM((n_dp, 16, 3 * per * 128), BF16),
                pltpu.VMEM((16, 3 * per * 128), F32),
                dma((4,)),
                dma((2, 2, half + 1)),
                dma((2, 2, half + 1)),
                dma((nz,)),
                dma((nz,)),
                dma((batches,)),
                dma((batches,)),
                dma((2, 2, half + 1)),
                dma((2, 2, half + 1)),
                dma((n_dp,)),
                dma((n_dp,)),
            ],
            compiler_params=pltpu.CompilerParams(
                collective_id=0, has_side_effects=True, vmem_limit_bytes=40 * 2**20
            ),
        )(expert_ids, gate_weights, tokens, cotangent, w_in, w_down)

    in_specs = (
        P(("dp", "expert"), None),
        P(("dp", "expert"), None),
        P(("dp", "expert"), None),
        P(("dp", "expert"), None),
        P(None, "expert", None),
        P("expert", None),
    )
    out_specs = (
        P(("dp", "expert"), None),
        P(("dp", "expert"), None),
        P(None, ("expert", "dp"), None),
        P(("expert", "dp"), None),
    )
    return jax.shard_map(
        step, mesh=mesh, in_specs=in_specs, out_specs=out_specs, check_vma=False
    )
```

time: 416 us -> 99.9 us (0.24)
  the two profiles are of different devices: /device:TPU:8 before, /device:TPU:2 now
where the time goes in v1:
time: 99.9 us; the launch traced here: 99.6 us
  Pallas kernels  91 us (91%)
  local copies, waits for them, and re-layouts  7.96 us (8%)
    pallas_call x1, Pallas kernels, step(): pl.pallas_call(functools.partial(moe_kernel, n_dp, nz), out_shape=(jax.Sh...  91 us
    unnamed x15, local copies, waits for them, and re-layouts  7.31 us

profile of v1, /device:TPU:2, one launch (start us, length us, event | category | flops | bytes accessed | tf_op | source)
XLA Modules:
  0.0 99.6 jit_solution(11577420907098687132)
XLA Ops:
  0.6 0.0 copy-start.4
  0.6 0.8 copy.10.ids_ref
  1.4 0.0 copy-done.4
  1.4 0.1 copy.11.gates_ref
  1.5 0.0 copy-start
  1.5 1.1 %copy-done = bf16[2,96,2048]{2,1,0:T(8,128)(2,1)S(1)} copy-done((bf16[2,96,2048]{2,1,0:T(8,128)(2,1)S(1)}, bf16[2,96,2048]{2,1,0:T(8,128)(2,1)}, u32[]{:S(2)}) %copy-start) | copy-done | bytes 786456
  2.7 0.0 copy-start.1
  2.7 1.0 %copy-done.1 = bf16[128,2048]{1,0:T(8,128)(2,1)S(1)} copy-done((bf16[128,2048]{1,0:T(8,128)(2,1)S(1)}, bf16[128,2048]{1,0:T(8,128)(2,1)}, u32[]{:S(2)}) %copy-start.1) | copy-done | bytes 524312
  3.7 0.0 copy-start.2
  3.7 1.0 %copy-done.2 = bf16[128,2048]{1,0:T(8,128)(2,1)S(1)} copy-done((bf16[128,2048]{1,0:T(8,128)(2,1)S(1)}, bf16[128,2048]{1,0:T(8,128)(2,1)}, u32[]{:S(2)}) %copy-start.2) | copy-done | bytes 524312
  4.8 0.0 copy-start.3
  4.8 1.0 copy-done.3
  5.8 91.0 %shard_map.93 = (bf16[128,2048]{1,0:T(8,128)(2,1)S(1)}, bf16[128,2048]{1,0:T(8,128)(2,1)S(1)}, f32[2,3,2048]{2,1,0:T(4,128)S(1)}, f32[3,2048]{1,0:T(4,128)S(1)}) custom-call(s32[128,8]{1,0:T(8,128)S(1)} %copy.10.ids_ref, f32[128,8]{1,0:T(8,128)S(1)} %copy.11.gates_ref, bf16[128,2048]{1,0:T(8,128)(2,1)S(1)} %copy-done.1, bf16[128,2048]{1,0:T(8,128)(2,1)S(1)} %copy-done.2, ...), custom_call_target="tpu_custom_call" | custom-call | tf_op jit(solution)/shard_map/pallas_call | solution.py:459
  96.7 0.7 copy.12
  97.4 0.8 copy.16
  98.2 0.8 copy.17
  99.0 0.6 copy.18
Async XLA Ops:
  0.6 0.8 copy-start.4
  1.5 1.1 %copy-start = (bf16[2,96,2048]{2,1,0:T(8,128)(2,1)S(1)}, bf16[2,96,2048]{2,1,0:T(8,128)(2,1)}, u32[]{:S(2)}) copy-start(bf16[2,96,2048]{2,1,0:T(8,128)(2,1)} %win_hbm.1) | copy-start | bytes 2359300
  2.7 1.0 %copy-start.1 = (bf16[128,2048]{1,0:T(8,128)(2,1)S(1)}, bf16[128,2048]{1,0:T(8,128)(2,1)}, u32[]{:S(2)}) copy-start(bf16[128,2048]{1,0:T(8,128)(2,1)} %tok_hbm.1) | copy-start | bytes 1572868
  3.7 1.0 %copy-start.2 = (bf16[128,2048]{1,0:T(8,128)(2,1)S(1)}, bf16[128,2048]{1,0:T(8,128)(2,1)}, u32[]{:S(2)}) copy-start(bf16[128,2048]{1,0:T(8,128)(2,1)} %cot_hbm.1) | copy-start | bytes 1572868
  4.8 1.0 %copy-start.3 = (bf16[96,2048]{1,0:T(8,128)(2,1)S(1)}, bf16[96,2048]{1,0:T(8,128)(2,1)}, u32[]{:S(2)}) copy-start(bf16[96,2048]{1,0:T(8,128)(2,1)} %wdn_hbm.1) | copy-start | bytes 1179652

commit v2 on v1

v2 whole, which is shorter than its diff:
```python
import functools

import jax
import jax.numpy as jnp
from jax import lax
from jax.experimental import pallas as pl
from jax.experimental.pallas import tpu as pltpu
from jax.sharding import PartitionSpec as P

MESH = pl.DeviceIdType.MESH
F32 = jnp.float32
BF16 = jnp.bfloat16
NT = (((1,), (1,)), ((), ()))
SPLITS = 2
TN = (((0,), (0,)), ((), ()))


def moe_kernel(
    n_dp, nz,
    ids_ref, gates_ref, tok_hbm, cot_hbm, win_hbm, wdn_hbm,
    rows_ref, pick_ref, acc9,
    tok, cot, win, wdn, x, pre, p32, q, qr, sb, rb, fin, g32, g, rg,
    in_sem, ag_send, ag_recv, far_send, sib_send, sib_recv, q_send, q_recv,
    back_send, rs_recv, fin_recv, g_send, g_recv,
):
    half = nz // 2
    feats = tok.shape[1]
    blocks = feats // 128
    hid = wdn.shape[0]
    per = hid // n_dp
    ntok = tok.shape[0]
    dp = lax.axis_index("dp")
    ex = lax.axis_index("expert")
    z = lax.div(ex, 2)
    core = lax.rem(ex, 2)
    zz = lax.rem(z, half)
    zl = half - 1 - zz
    held = lax.div(z, half)
    sib = (dp, z * 2 + 1 - core)

    loads = [
        pltpu.make_async_copy(tok_hbm, tok, in_sem.at[0]),
        pltpu.make_async_copy(cot_hbm, cot, in_sem.at[1]),
        pltpu.make_async_copy(win_hbm, win, in_sem.at[2]),
        pltpu.make_async_copy(wdn_hbm, wdn, in_sem.at[3]),
    ]
    for load in loads:
        load.start()

    barrier = pltpu.get_barrier_semaphore()
    pl.semaphore_signal(barrier, inc=1, device_id=sib, device_id_type=MESH)

    @pl.loop(1, nz)
    def _(k):
        pl.semaphore_signal(
            barrier, inc=1, device_id=(dp, lax.rem(z + k, nz) * 2 + core), device_id_type=MESH
        )

    @pl.loop(1, n_dp)
    def _(k):
        pl.semaphore_signal(
            barrier, inc=1, device_id=(lax.rem(dp + k, n_dp), ex), device_id_type=MESH
        )

    ids = ids_ref[...]
    gates = gates_ref[...]
    after = lax.broadcasted_iota(jnp.int32, (ntok, ntok), 1)
    before = lax.broadcasted_iota(jnp.int32, (ntok, ntok), 0)
    tri = jnp.where(before < after, 1.0, 0.0).astype(BF16)
    slot = lax.broadcasted_iota(jnp.int32, (8, ntok), 0).astype(F32)
    picks = []
    scales = []
    for e in range(2):
        hit = ids == e
        chosen = jnp.max(jnp.where(hit, 1.0, 0.0), axis=0, keepdims=True)
        weight = jnp.sum(jnp.where(hit, gates, 0.0), axis=0, keepdims=True)
        chosen = jnp.broadcast_to(chosen, (8, ntok))
        rank = jnp.dot(
            jnp.concatenate([chosen, chosen], axis=0).astype(BF16), tri,
            preferred_element_type=F32,
        )[0:8]
        pick = jnp.where((chosen > 0.5) & (rank == slot), 1.0, 0.0)
        picks.append(pick)
        scales.append(jnp.sum(pick * weight, axis=1, keepdims=True))
    pick = jnp.concatenate(picks, axis=0).astype(BF16)
    scale = jnp.concatenate(scales, axis=0)

    loads[0].wait()
    tok_rows = jnp.dot(pick, tok[...], preferred_element_type=F32)
    loads[1].wait()
    cot_rows = jnp.dot(pick, cot[...], preferred_element_type=F32) * scale
    packet = [
        jnp.concatenate([tok_rows[8 * e:8 * e + 8], cot_rows[8 * e:8 * e + 8]], axis=0)
        for e in range(2)
    ]
    first = held == 0
    x[0, 0] = jnp.where(first, packet[0], packet[1]).astype(BF16)
    x[0, nz] = jnp.where(first, packet[1], packet[0]).astype(BF16)

    pl.semaphore_wait(barrier, nz + n_dp - 1)

    def slot_of(d, i):
        return 0 if i == 0 else (2 * i - 1 if d == 0 else 2 * i)

    steps = (half, half - 1)
    edge = (zz, zl)
    wide = feats // SPLITS

    def cols(h):
        return pl.ds(h * wide, wide)

    def away(d, i):
        return (dp, lax.rem(z + (i if d == 0 else nz - i), nz) * 2 + core)

    def remote(src, dst, send, recv, dev):
        return pltpu.make_async_remote_copy(
            src_ref=src, dst_ref=dst, send_sem=send, recv_sem=recv,
            device_id=dev, device_id_type=MESH,
        )

    def start(copy):
        copy.start()

    def wait_send(copy):
        copy.wait_send()

    def passes(d):
        return edge[d] <= half - 2

    def ag_chain(d, i, h, act):
        @pl.when(passes(d))
        def _():
            act(remote(
                x.at[0, slot_of(d, i), :, cols(h)], x.at[0, slot_of(d, i + 1), :, cols(h)],
                ag_send.at[d, i, h], ag_recv.at[d, i + 1, h], away(d, 1),
            ))

    def ag_direct(d, i, h):
        at = 2 * i - 1 if d == 0 else 2 * i
        return remote(
            x.at[0, nz, :, cols(h)], x.at[0, at, :, cols(h)],
            far_send.at[d, h], ag_recv.at[d, i, h], away(d, i),
        )

    def ag_export(d, h, act):
        dist = half - edge[d]

        @pl.when(dist <= steps[d])
        def _():
            act(ag_direct(d, dist, h))

    def ag_wait(d, i, h):
        at = x.at[0, slot_of(d, i), :, cols(h)]
        remote(at, at, ag_send.at[d, i, h], ag_recv.at[d, i, h], away(d, 1)).wait_recv()

    def sib_copy(s):
        return remote(x.at[0, s], x.at[1, s], sib_send.at[s], sib_recv.at[s], sib)

    per_batch = 4 if nz % 4 == 0 else 2
    batches = nz // per_batch
    rows = per_batch * 16

    def stage_one(b):
        lo = b * per_batch
        for s in range(lo, lo + per_batch):
            sib_copy(s).wait_recv()
        xb = x[0:2, lo:lo + per_batch].reshape(2 * rows, feats)
        gate = lax.dot_general(xb, win[0], NT, preferred_element_type=F32)
        up = lax.dot_general(xb, win[1], NT, preferred_element_type=F32)
        grad = lax.dot_general(xb, wdn[...], NT, preferred_element_type=F32)
        gate = gate.reshape(2 * per_batch, 16, hid)[:, 0:8]
        up = up.reshape(2 * per_batch, 16, hid)[:, 0:8]
        grad = grad.reshape(2 * per_batch, 16, hid)[:, 8:16]
        sig = 1.0 / (1.0 + jnp.exp(-gate))
        silu = gate * sig
        hidden = silu * up
        grad_gate = grad * up * (sig * (1.0 + gate * (1.0 - sig)))
        grad_up = grad * silu
        zero = jnp.zeros_like(hidden)
        for k, pair in enumerate(
            ((grad_gate, zero), (grad_up, zero), (zero, hidden))
        ):
            both = jnp.concatenate(pair, axis=1).astype(BF16)
            pre[k, 0:2, lo:lo + per_batch] = both.reshape(2, per_batch, 16, hid)
        for k, pair in enumerate(
            ((zero, grad_gate), (zero, grad_up), (hidden, zero))
        ):
            both = jnp.concatenate(pair, axis=1).astype(BF16)
            pre[3 + k, 0:2, lo:lo + per_batch] = both.reshape(2, per_batch, 16, hid)

    for h in range(SPLITS):
        for d in (0, 1):
            ag_chain(d, 0, h, start)

    def export_at(d, when):
        @pl.when(when)
        def _():
            for h in range(SPLITS):
                ag_export(d, h, start)

    for d in (0, 1):
        export_at(d, edge[d] >= half - 2)
    sib_copy(0).start()
    for load in loads[2:]:
        load.wait()
    done = 0
    for i in range(1, half + 1):
        for h in range(SPLITS):
            for d in (0, 1):
                if i <= steps[d]:
                    ag_wait(d, i, h)
                    if i < steps[d]:
                        ag_chain(d, i, h, start)
        for d in (0, 1):
            if 2 * i < half:
                export_at(
                    d, (edge[d] < half - 2 * i) & (edge[d] >= half - 2 - 2 * i)
                )
        for d in (0, 1):
            if i <= steps[d]:
                sib_copy(slot_of(d, i)).start()
        if i < half and 2 * i - 1 >= (done + 1) * per_batch:
            stage_one(done)
            done += 1
    while done < batches:
        stage_one(done)
        done += 1

    def q_copy(b):
        at = pl.ds(b * per_batch, per_batch)
        return remote(q.at[at], qr.at[at], q_send.at[b], q_recv.at[b], sib)

    def stage_two(b):
        lo = b * per_batch
        for c in (1, 0):
            total = None
            for k, w in enumerate((win.at[0], win.at[1], wdn)):
                lhs = pre[3 + k, c, lo:lo + per_batch].reshape(rows, hid)
                term = jnp.dot(lhs, w[...], preferred_element_type=F32)
                total = term if total is None else total + term
            total = total.reshape(per_batch, 16, feats)
            if c == 1:
                q[lo:lo + per_batch] = total.astype(BF16)
                q_copy(b).start()
            else:
                p32[lo:lo + per_batch] = total

    def rs_send(d, i, h, act):
        src = sb.at[slot_of(d, i), :, cols(h)]
        def final(kind):
            return remote(
                src, fin.at[d, kind, :, cols(h)],
                back_send.at[d, i, h], fin_recv.at[d, kind, h], away(1 - d, i),
            )

        @pl.when(edge[d] == 0)
        def _():
            act(final(1))

        @pl.when(edge[d] != 0)
        def _():
            if i == 1:
                act(final(0))
            else:
                act(remote(
                    src, rb.at[d, i - 1, :, cols(h)],
                    back_send.at[d, i, h], rs_recv.at[d, i - 1, h], away(1 - d, 1),
                ))

    def chain(d, i, h):
        slot = slot_of(d, i)
        at = cols(h)
        if i < steps[d]:
            has = passes(d)

            @pl.when(has)
            def _():
                here = rb.at[d, i, :, at]
                remote(
                    here, here, back_send.at[d, i, h], rs_recv.at[d, i, h], away(1 - d, 1)
                ).wait_recv()
                sb[slot, :, at] = (p32[slot, :, at] + rb[d, i, :, at].astype(F32)).astype(BF16)

            @pl.when(jnp.logical_not(has))
            def _():
                sb[slot, :, at] = p32[slot, :, at].astype(BF16)
        else:
            sb[slot, :, at] = p32[slot, :, at].astype(BF16)
        rs_send(d, i, h, start)

    def g_copy(k):
        peer = lax.rem(dp + k, n_dp)
        return pltpu.make_async_remote_copy(
            src_ref=g.at[peer],
            dst_ref=rg.at[k],
            send_sem=g_send.at[k],
            recv_sem=g_recv.at[k],
            device_id=(peer, ex),
            device_id_type=MESH,
        )

    def g_block(n):
        at = pl.ds(pl.multiple_of(n * 16, 16), 16)
        return jnp.concatenate([g32[kj, at, :] for kj in range(3 * per)], axis=1)

    def weight_grads():
        unit = lax.broadcasted_iota(jnp.int32, (hid, hid), 1)
        row = lax.broadcasted_iota(jnp.int32, (hid, hid), 0)
        want = lax.rem(row, n_dp) * per + lax.div(row, n_dp)
        perm = jnp.where(unit == want, 1.0, 0.0).astype(BF16)
        lhs = jnp.concatenate(
            [
                lax.dot_general(
                    perm, pre[k].reshape(2 * nz * 16, hid), NT, preferred_element_type=F32
                )
                for k in range(3)
            ],
            axis=0,
        ).astype(BF16)
        for r2 in range(blocks // 2):
            xs = x[0:2, 0:nz, :, 256 * r2:256 * r2 + 256].reshape(2 * nz * 16, 256)
            term = jnp.dot(lhs, xs, preferred_element_type=F32)
            for r in (0, 1):
                for kj in range(3 * per):
                    g32[kj, pl.ds(2 * r2 + r, n_dp, stride=16), :] = term[
                        kj * n_dp:kj * n_dp + n_dp, 128 * r:128 * r + 128
                    ]

        @pl.loop(1, n_dp)
        def _(k):
            peer = lax.rem(dp + k, n_dp)
            g[peer] = g_block(peer).astype(BF16)
            g_copy(k).start()

    pending = list(range(batches - 1, -1, -1))
    arrived = batches

    def next_stage():
        if pending:
            stage_two(pending.pop(0))

    next_stage()
    next_stage()
    for j in range(1, half + 1):
        hops = [(d, (half + 1 if d == 0 else half) - j) for d in (0, 1)]
        hops = [(d, i) for d, i in hops if i >= 1]
        low = min(slot_of(d, i) for d, i in hops)
        while arrived * per_batch > low:
            arrived -= 1
            if arrived in pending:
                next_stage()
            q_copy(arrived).wait_recv()
            at = pl.ds(arrived * per_batch, per_batch)
            p32[at] = p32[at] + qr[at].astype(F32)
        for h in range(SPLITS):
            for d, i in hops:
                chain(d, i, h)
        if j == 1:
            weight_grads()
        else:
            next_stage()
    while arrived > 0:
        arrived -= 1
        q_copy(arrived).wait_recv()
        at = pl.ds(arrived * per_batch, per_batch)
        p32[at] = p32[at] + qr[at].astype(F32)

    acc9[...] = g_block(dp)

    @pl.loop(1, n_dp)
    def _(k):
        g_copy(k).wait_recv()
        acc9[...] += rg[k].astype(F32)

    p32[1] = jnp.zeros((16, feats), F32)

    def take(d, kind):
        for h in range(SPLITS):
            here = fin.at[d, kind, :, cols(h)]
            remote(
                here, here, back_send.at[d, 1, h], fin_recv.at[d, kind, h], away(1 - d, 1)
            ).wait_recv()
        p32[kind] = p32[kind] + fin[d, kind].astype(F32)

    for d in (0, 1):
        pl.when(half - edge[d] <= steps[d])(functools.partial(take, d, 1))
        pl.when(edge[d] <= half - 2)(functools.partial(take, d, 0))

    mine, theirs = p32[0], p32[1]
    sums = [jnp.where(first, mine, theirs), jnp.where(first, theirs, mine)]
    out_rows = jnp.concatenate([sums[0][0:8], sums[1][0:8]], axis=0) * scale
    grad_rows = jnp.concatenate([sums[0][8:16], sums[1][8:16]], axis=0)
    rows_ref[0:16] = out_rows.astype(BF16)
    rows_ref[16:32] = grad_rows.astype(BF16)
    pick_ref[...] = pick

    for h in range(SPLITS):
        for d in (0, 1):
            ag_export(d, h, wait_send)
            for i in range(steps[d]):
                ag_chain(d, i, h, wait_send)
                rs_send(d, i + 1, h, wait_send)
    for s in range(nz):
        sib_copy(s).wait_send()
    for b in range(batches):
        q_copy(b).wait_send()

    @pl.loop(1, n_dp)
    def _(k):
        g_copy(k).wait_send()


def place_kernel(rows_ref, pick_ref, acc9, out_ref, gtok_ref, gwin_ref, gwdn_ref):
    pick = pick_ref[...]
    for ref, rows in ((out_ref, rows_ref[0:16]), (gtok_ref, rows_ref[16:32])):
        ref[...] = lax.dot_general(pick, rows, TN, preferred_element_type=F32).astype(BF16)
    per = gwdn_ref.shape[0]
    for kj in range(3 * per):
        kind, j = kj // per, kj % per
        for r in range(16):
            line = acc9[r:r + 1, kj * 128:kj * 128 + 128]
            if kind < 2:
                gwin_ref[j, kind:kind + 1, r * 128:r * 128 + 128] = line
            else:
                gwdn_ref[j:j + 1, r * 128:r * 128 + 128] = line


def solution(mesh):
    n_dp = mesh.shape["dp"]
    nz = mesh.shape["expert"] // 2

    def step(tokens, expert_ids, gate_weights, cotangent, w_in, w_down):
        ntok, feats = tokens.shape
        hid = w_down.shape[0]
        per = hid // n_dp
        half = nz // 2
        batches = nz // (4 if nz % 4 == 0 else 2)
        vmem = pl.BlockSpec(memory_space=pltpu.VMEM)
        hbm = pl.BlockSpec(memory_space=pl.ANY)
        dma = pltpu.SemaphoreType.DMA
        rows, pick, sums = pl.pallas_call(
            functools.partial(moe_kernel, n_dp, nz),
            out_shape=(
                jax.ShapeDtypeStruct((32, feats), BF16),
                jax.ShapeDtypeStruct((16, ntok), BF16),
                jax.ShapeDtypeStruct((16, 3 * per * 128), F32),
            ),
            in_specs=[vmem, vmem, hbm, hbm, hbm, hbm],
            out_specs=(vmem, vmem, vmem),
            scratch_shapes=[
                pltpu.VMEM((ntok, feats), BF16),
                pltpu.VMEM((ntok, feats), BF16),
                pltpu.VMEM((2, hid, feats), BF16),
                pltpu.VMEM((hid, feats), BF16),
                pltpu.VMEM((2, nz + 1, 16, feats), BF16),
                pltpu.VMEM((6, 2, nz, 16, hid), BF16),
                pltpu.VMEM((nz, 16, feats), F32),
                pltpu.VMEM((nz, 16, feats), BF16),
                pltpu.VMEM((nz, 16, feats), BF16),
                pltpu.VMEM((nz, 16, feats), BF16),
                pltpu.VMEM((2, half, 16, feats), BF16),
                pltpu.VMEM((2, 2, 16, feats), BF16),
                pltpu.VMEM((3 * per, n_dp * 16, 128), F32),
                pltpu.VMEM((n_dp, 16, 3 * per * 128), BF16),
                pltpu.VMEM((n_dp, 16, 3 * per * 128), BF16),
                dma((4,)),
                dma((2, half, SPLITS)),
                dma((2, half + 1, SPLITS)),
                dma((2, SPLITS)),
                dma((nz,)),
                dma((nz,)),
                dma((batches,)),
                dma((batches,)),
                dma((2, half + 1, SPLITS)),
                dma((2, half, SPLITS)),
                dma((2, 2, SPLITS)),
                dma((n_dp,)),
                dma((n_dp,)),
            ],
            compiler_params=pltpu.CompilerParams(
                collective_id=0, has_side_effects=True, vmem_limit_bytes=62 * 2**20
            ),
        )(expert_ids.T, gate_weights.T, tokens, cotangent, w_in, w_down)
        out, grad, grad_in, grad_down = pl.pallas_call(
            place_kernel,
            out_shape=(
                jax.ShapeDtypeStruct((ntok, feats), BF16),
                jax.ShapeDtypeStruct((ntok, feats), BF16),
                jax.ShapeDtypeStruct((per, 2, feats), F32),
                jax.ShapeDtypeStruct((per, feats), F32),
            ),
            in_specs=[vmem, vmem, vmem],
            out_specs=(vmem, vmem, vmem, vmem),
        )(rows, pick, sums)
        return out, grad, jnp.transpose(grad_in, (1, 0, 2)), grad_down

    in_specs = (
        P(("dp", "expert"), None),
        P(("dp", "expert"), None),
        P(("dp", "expert"), None),
        P(("dp", "expert"), None),
        P(None, "expert", None),
        P("expert", None),
    )
    out_specs = (
        P(("dp", "expert"), None),
        P(("dp", "expert"), None),
        P(None, ("expert", "dp"), None),
        P(("expert", "dp"), None),
    )
    return jax.shard_map(
        step, mesh=mesh, in_specs=in_specs, out_specs=out_specs, check_vma=False
    )
```

time: 99.9 us -> 89.7 us (0.90)
  the two profiles are of different devices: /device:TPU:2 before, /device:TPU:134 now
where the time goes in v2:
time: 89.7 us; the launch traced here: 89.5 us
  Pallas kernels  88.9 us (99%)
    pallas_call x1, Pallas kernels, step(): pl.pallas_call(functools.partial(moe_kernel, n_dp, nz), out_shape=(jax.Sh...  86.6 us
    pallas_call x1, Pallas kernels, step(): pl.pallas_call(place_kernel, out_shape=(jax.ShapeDtypeStruct((ntok, feats...  2.26 us

profile of v2, /device:TPU:134, one launch (start us, length us, event | category | flops | bytes accessed | tf_op | source)
XLA Modules:
  0.0 89.5 jit_solution(8421593765127618892)
XLA Ops:
  0.6 86.6 %shard_map.93 = (bf16[32,2048]{1,0:T(8,128)(2,1)}, bf16[16,128]{1,0:T(8,128)(2,1)}, f32[16,1152]{1,0:T(8,128)}) custom-call(s32[8,128]{1,0:T(8,128)} %bitcast.3, f32[8,128]{1,0:T(8,128)} %bitcast.4, bf16[128,2048]{1,0:T(8,128)(2,1)} %tok_hbm.1, bf16[128,2048]{1,0:T(8,128)(2,1)} %cot_hbm.1, bf16[2,96,2048]{2,1,0:T(8,128)(2,1)} %win_hbm.1, ...), custom_call_target="tpu_custom_call" | custom-call | tf_op jit(solution)/shard_map/pallas_call | solution.py:441
  87.3 2.3 %shard_map.94 = (bf16[128,2048]{1,0:T(8,128)(2,1)}, bf16[128,2048]{1,0:T(8,128)(2,1)}, f32[3,2,2048]{2,1,0:T(2,128)}, f32[3,2048]{1,0:T(4,128)}) custom-call(bf16[32,2048]{1,0:T(8,128)(2,1)} %get-tuple-element.11.rows_ref, bf16[16,128]{1,0:T(8,128)(2,1)} %get-tuple-element.12.pick_ref, f32[16,1152]{1,0:T(8,128)} %get-tuple-element.13.acc9), custom_call_target="tpu_custom_call" | custom-call | tf_op jit(solution)/shard_map/pallas_call | solution.py:484

commit v3 on v2

--- a/solution.py
+++ b/solution.py
@@ -156,7 +156,7 @@
     def sib_copy(s):
         return remote(x.at[0, s], x.at[1, s], sib_send.at[s], sib_recv.at[s], sib)
 
-    per_batch = 4 if nz % 4 == 0 else 2
+    per_batch = 2
     batches = nz // per_batch
     rows = per_batch * 16
 
@@ -434,7 +434,7 @@
         hid = w_down.shape[0]
         per = hid // n_dp
         half = nz // 2
-        batches = nz // (4 if nz % 4 == 0 else 2)
+        batches = nz // 2
         vmem = pl.BlockSpec(memory_space=pltpu.VMEM)
         hbm = pl.BlockSpec(memory_space=pl.ANY)
         dma = pltpu.SemaphoreType.DMA

time: 89.7 us -> 89.1 us (level)
  no operation moved by 1% of the time
where the time goes in v3:
time: 89.1 us; the launch traced here: 88.9 us
  Pallas kernels  88.3 us (99%)
    pallas_call x1, Pallas kernels, step(): pl.pallas_call(functools.partial(moe_kernel, n_dp, nz), out_shape=(jax.Sh...  86 us
    pallas_call x1, Pallas kernels, step(): pl.pallas_call(place_kernel, out_shape=(jax.ShapeDtypeStruct((ntok, feats...  2.26 us

profile of v3, /device:TPU:134, one launch (start us, length us, event | category | flops | bytes accessed | tf_op | source)
XLA Modules:
  0.0 88.9 jit_solution(5582659072844563518)
XLA Ops:
  0.6 86.0 %shard_map.93 = (bf16[32,2048]{1,0:T(8,128)(2,1)}, bf16[16,128]{1,0:T(8,128)(2,1)}, f32[16,1152]{1,0:T(8,128)}) custom-call(s32[8,128]{1,0:T(8,128)} %bitcast.3, f32[8,128]{1,0:T(8,128)} %bitcast.4, bf16[128,2048]{1,0:T(8,128)(2,1)} %tok_hbm.1, bf16[128,2048]{1,0:T(8,128)(2,1)} %cot_hbm.1, bf16[2,96,2048]{2,1,0:T(8,128)(2,1)} %win_hbm.1, ...), custom_call_target="tpu_custom_call" | custom-call | tf_op jit(solution)/shard_map/pallas_call | solution.py:441
  86.6 2.3 %shard_map.94 = (bf16[128,2048]{1,0:T(8,128)(2,1)}, bf16[128,2048]{1,0:T(8,128)(2,1)}, f32[3,2,2048]{2,1,0:T(2,128)}, f32[3,2048]{1,0:T(4,128)}) custom-call(bf16[32,2048]{1,0:T(8,128)(2,1)} %get-tuple-element.11.rows_ref, bf16[16,128]{1,0:T(8,128)(2,1)} %get-tuple-element.12.pick_ref, f32[16,1152]{1,0:T(8,128)} %get-tuple-element.13.acc9), custom_call_target="tpu_custom_call" | custom-call | tf_op jit(solution)/shard_map/pallas_call | solution.py:484
